TPU v7x, 512 devices: a whole 4x4x16 slice. The times are simulated.
512 devices in a mesh: cuts: 32 (over z, x_lo), blk: 16 (over x_hi, y, core).
Axes of the slice: x: 4 (x_hi: 2, x_lo: 2; x = x_hi * 2 + x_lo), y: 4, z: 16, core: 2. Of those that a mesh axis runs over, the one named last changes fastest.
Arguments:
- steps: bfloat16 [512, 2, 512, 512], P(('cuts', 'blk')), as said below
Outputs:
- sidebands: float32 [32, 2, 512, 512], P(None, None, 'blk', 'cuts')
Inputs may be any that keep to these rules, and one draw needn't show every extreme that they name: `steps`: sqrt(512) times every entry lies between -1 and 1.
All inputs are finite; a program needn't handle non-finite values.
Results may differ from a plain program's by a relative error of at most 0.035.
Values may be sent and summed in bfloat16 or wider, within the bound.
A program may use at most 64 MiB of HBM per device.

v0:
```python
import math
import jax
import jax.numpy as jnp
from jax import lax
from jax.sharding import PartitionSpec as P


def from_partner(block, axis, distance):
    count = lax.axis_size(axis)
    route = []
    for low in range(count):
        high = low | 1 << distance
        if high != low and high < count:
            route += [(low, high), (high, low)]
    return lax.ppermute(block, axis, route)


def passed_along(x, axis, by):
    devices = lax.axis_size(axis)
    return lax.ppermute(x, axis, [(i, (i + by) % devices) for i in range(devices)])


def complex_product(left_factor, right_factor):
    real_real = jnp.dot(left_factor[0], right_factor[0], preferred_element_type=jnp.float32)
    imag_imag = jnp.dot(left_factor[1], right_factor[1], preferred_element_type=jnp.float32)
    real_imag = jnp.dot(left_factor[0], right_factor[1], preferred_element_type=jnp.float32)
    imag_real = jnp.dot(left_factor[1], right_factor[0], preferred_element_type=jnp.float32)
    return jnp.stack([real_real - imag_imag, real_imag + imag_real])


def complex_wide(left_factor, right_factor):
    hp = lax.Precision.HIGHEST
    real_real = jnp.dot(left_factor[0], right_factor[0], precision=hp)
    imag_imag = jnp.dot(left_factor[1], right_factor[1], precision=hp)
    real_imag = jnp.dot(left_factor[0], right_factor[1], precision=hp)
    imag_real = jnp.dot(left_factor[1], right_factor[0], precision=hp)
    return jnp.stack([real_real - imag_imag, real_imag + imag_real])


def group_product(left_factor, right_factor):
    if left_factor.dtype == jnp.bfloat16:
        return complex_product(left_factor, right_factor)
    return complex_wide(left_factor, right_factor)


def per_device(steps):
    current = steps[0]
    order = current.shape[-1]
    blk_count = lax.axis_size("blk")
    block_rows = order // blk_count
    tree_depth = blk_count.bit_length() - 1
    blk_index = lax.axis_index("blk")
    first_partner = from_partner(current, "blk", 0)
    for section in range(tree_depth):
        if section == 0:
            partner = first_partner
        else:
            partner = from_partner(current, "blk", section)
        is_upper = blk_index >> section & 1 == 1
        upper_factor = jnp.where(is_upper, current, partner)
        lower_factor = jnp.where(is_upper, partner, current)
        current = group_product(upper_factor, lower_factor)
    current = current.astype(jnp.bfloat16)
    row_block = lax.dynamic_slice_in_dim(current, blk_index * block_rows, block_rows, 1)
    cuts_count = lax.axis_size("cuts")
    loop_depth = cuts_count.bit_length() - 1
    for section in range(loop_depth):
        distance = 1 << section
        ahead = passed_along(row_block, "cuts", -distance)

        def add_rows(running, incoming, offset, ahead=ahead):
            return complex_product(ahead, incoming)

        empty_sum = jnp.zeros(row_block.shape, jnp.float32)
        running = add_rows(
            empty_sum, lax.all_gather(row_block, "blk", axis=1, tiled=True), jnp.int32(0)
        )
        row_block = running.astype(jnp.bfloat16)
    received = lax.all_to_all(row_block[None], "cuts", split_axis=3, concat_axis=0, tiled=True)
    slice_count = received.shape[0]
    freq_index = jnp.arange(slice_count, dtype=jnp.int32)
    phase_angle = (
        2.0
        * math.pi
        / slice_count
        * (freq_index[:, None] * freq_index[None, :] % slice_count).astype(jnp.float32)
    )
    cosine_table = jnp.cos(phase_angle)
    sine_table = jnp.sin(phase_angle)
    flattened = received.astype(jnp.float32).reshape(slice_count, 2, -1)
    hp = lax.Precision.HIGHEST
    real_part = jnp.dot(cosine_table, flattened[:, 0], precision=hp) + jnp.dot(
        sine_table, flattened[:, 1], precision=hp
    )
    imag_part = jnp.dot(cosine_table, flattened[:, 1], precision=hp) - jnp.dot(
        sine_table, flattened[:, 0], precision=hp
    )
    norm_factor = math.sqrt(order / slice_count)
    result = jnp.stack([real_part, imag_part], axis=1) * norm_factor
    return result.reshape(received.shape)


def solution(mesh):
    in_specs = (P(("cuts", "blk"), None, None, None),)
    out_specs = P(None, None, "blk", "cuts")
    return jax.shard_map(
        per_device, mesh=mesh, in_specs=in_specs, out_specs=out_specs, check_vma=False
    )
```

profile of v0, /device:TPU:2, one launch (start us, length us, event | category | flops | bytes accessed | tf_op | source)
XLA Modules:
  0.0 564.4 jit_solution(16650119582925848394)
XLA Ops:
  8.5 2.8 collective-permute-done
  15.9 3.5 collective-permute-start.1
  19.4 46.4 %collective-permute-done.1 = f32[2,512,512]{2,1,0:T(8,128)} collective-permute-done((f32[2,512,512]{2,1,0:T(8,128)}, f32[2,512,512]{2,1,0:T(8,128)}, u32[]{:S(2)}, u32[]{:S(2)}) %collective-permute-start.1) | collective-permute-done | bytes 2097184 | tf_op jit(solution)/shard_map/ppermute | solution.py:15
  65.8 2.3 broadcast_select_fusion.3
  77.1 5.3 collective-permute-start.2
  82.3 45.3 %collective-permute-done.2 = f32[2,512,512]{2,1,0:T(8,128)} collective-permute-done((f32[2,512,512]{2,1,0:T(8,128)}, f32[2,512,512]{2,1,0:T(8,128)}, u32[]{:S(2)}, u32[]{:S(2)}) %collective-permute-start.2) | collective-permute-done | bytes 2097184 | tf_op jit(solution)/shard_map/ppermute | solution.py:15
  127.6 2.3 broadcast_select_fusion.5
  138.9 4.2 collective-permute-start.3
  143.1 45.4 %collective-permute-done.3 = f32[2,512,512]{2,1,0:T(8,128)} collective-permute-done((f32[2,512,512]{2,1,0:T(8,128)}, f32[2,512,512]{2,1,0:T(8,128)}, u32[]{:S(2)}, u32[]{:S(2)}) %collective-permute-start.3) | collective-permute-done | bytes 2097184 | tf_op jit(solution)/shard_map/ppermute | solution.py:15
  188.5 2.3 broadcast_select_fusion.6
  199.1 7.8 %collective-permute-start.4 = (bf16[2,32,512]{2,1,0:T(8,128)(2,1)}, bf16[2,32,512]{2,1,0:T(8,128)(2,1)S(1)}, u32[]{:S(2)}, u32[]{:S(2)}) collective-permute-start(bf16[2,32,512]{2,1,0:T(8,128)(2,1)} %fusion.50), channel_id=1, source_target_pairs={{0,496},{16,0},{32,16},{48,32},{64,48},{80,64},{96,80},{112,96},{1... | collective-permute-start | bytes 196616 | tf_op jit(solution)/shard_map/ppermute | solution.py:20
  209.1 53.8 %all-gather.6.cloned.1.call-done = bf16[2,512,512]{2,1,0:T(8,128)(2,1)} async-done(((bf16[2,32,512]{2,1,0:T(8,128)(2,1)}), bf16[2,512,512]{2,1,0:T(8,128)(2,1)}) %all-gather.6.cloned.1.call-update) | async-done | bytes 1048592 | tf_op jit(solution)/shard_map/all_gather | solution.py:76
  268.6 6.0 %collective-permute-start.5 = (bf16[2,32,512]{2,1,0:T(8,128)(2,1)}, bf16[2,32,512]{2,1,0:T(8,128)(2,1)S(1)}, u32[]{:S(2)}, u32[]{:S(2)}) collective-permute-start(bf16[2,32,512]{2,1,0:T(8,128)(2,1)} %pad_maximum_fusion.3), channel_id=1, source_target_pairs={{0,480},{16,496},{32,0},{48,16},{64,32},{80,48},{96,64},{112,80},{... | collective-permute-start | bytes 196616 | tf_op jit(solution)/shard_map/ppermute | solution.py:20
  276.7 51.0 %all-gather.8.cloned.1.call-done = bf16[2,512,512]{2,1,0:T(8,128)(2,1)} async-done(((bf16[2,32,512]{2,1,0:T(8,128)(2,1)}), bf16[2,512,512]{2,1,0:T(8,128)(2,1)}) %all-gather.8.cloned.1.call-update) | async-done | bytes 1048592 | tf_op jit(solution)/shard_map/all_gather | solution.py:76
  333.3 6.8 %collective-permute-start.6 = (bf16[2,32,512]{2,1,0:T(8,128)(2,1)}, bf16[2,32,512]{2,1,0:T(8,128)(2,1)S(1)}, u32[]{:S(2)}, u32[]{:S(2)}) collective-permute-start(bf16[2,32,512]{2,1,0:T(8,128)(2,1)} %pad_maximum_fusion.4), channel_id=1, source_target_pairs={{0,448},{16,464},{32,480},{48,496},{64,0},{80,16},{96,32},{112,48}... | collective-permute-start | bytes 196616 | tf_op jit(solution)/shard_map/ppermute | solution.py:20
  340.1 3.5 collective-permute-done.6
  343.6 48.8 %all-gather.10.cloned.1.call-done = bf16[2,512,512]{2,1,0:T(8,128)(2,1)} async-done(((bf16[2,32,512]{2,1,0:T(8,128)(2,1)}), bf16[2,512,512]{2,1,0:T(8,128)(2,1)}) %all-gather.10.cloned.1.call-update) | async-done | bytes 1048592 | tf_op jit(solution)/shard_map/all_gather | solution.py:76
  398.1 8.4 %collective-permute-start.7 = (bf16[2,32,512]{2,1,0:T(8,128)(2,1)}, bf16[2,32,512]{2,1,0:T(8,128)(2,1)S(1)}, u32[]{:S(2)}, u32[]{:S(2)}) collective-permute-start(bf16[2,32,512]{2,1,0:T(8,128)(2,1)} %pad_maximum_fusion.5), channel_id=1, source_target_pairs={{0,384},{16,400},{32,416},{48,432},{64,448},{80,464},{96,480},{112... | collective-permute-start | bytes 196616 | tf_op jit(solution)/shard_map/ppermute | solution.py:20
  406.5 6.3 %collective-permute-done.7 = bf16[2,32,512]{2,1,0:T(8,128)(2,1)S(1)} collective-permute-done((bf16[2,32,512]{2,1,0:T(8,128)(2,1)}, bf16[2,32,512]{2,1,0:T(8,128)(2,1)S(1)}, u32[]{:S(2)}, u32[]{:S(2)}) %collective-permute-start.7) | collective-permute-done | bytes 65568 | tf_op jit(solution)/shard_map/ppermute | solution.py:20
  412.8 44.4 %all-gather.12.cloned.1.call-done = bf16[2,512,512]{2,1,0:T(8,128)(2,1)} async-done(((bf16[2,32,512]{2,1,0:T(8,128)(2,1)}), bf16[2,512,512]{2,1,0:T(8,128)(2,1)}) %all-gather.12.cloned.1.call-update) | async-done | bytes 1048592 | tf_op jit(solution)/shard_map/all_gather | solution.py:76
  462.9 12.8 %collective-permute-start.8 = (bf16[2,32,512]{2,1,0:T(8,128)(2,1)}, bf16[2,32,512]{2,1,0:T(8,128)(2,1)S(1)}, u32[]{:S(2)}, u32[]{:S(2)}) collective-permute-start(bf16[2,32,512]{2,1,0:T(8,128)(2,1)} %pad_maximum_fusion.6), channel_id=1, source_target_pairs={{0,256},{16,272},{32,288},{48,304},{64,320},{80,336},{96,352},{112... | collective-permute-start | bytes 196616 | tf_op jit(solution)/shard_map/ppermute | solution.py:20
  475.7 3.0 collective-permute-done.8
  478.7 43.3 %all-gather.14.cloned.1.call-done = bf16[2,512,512]{2,1,0:T(8,128)(2,1)} async-done(((bf16[2,32,512]{2,1,0:T(8,128)(2,1)}), bf16[2,512,512]{2,1,0:T(8,128)(2,1)}) %all-gather.14.cloned.1.call-update) | async-done | bytes 1048592 | tf_op jit(solution)/shard_map/all_gather | solution.py:76
  527.4 27.2 %all_to_all.15 = bf16[32,2,512]{2,1,0:T(2,128)(2,1)S(1)} all-to-all(bf16[32,2,512]{2,1,0:T(2,128)(2,1)S(1)} %reshape.43), channel_id=1, replica_groups=mesh['cuts'=32,'blk'=16] {'cuts'}, dimensions={0} | all-to-all | bytes 131072 | tf_op jit(solution)/shard_map/all_to_all | solution.py:79
  (72 shorter events, 68.0 us)
Async XLA Ops:
  6.5 256.4 %all-gather.6.cloned.1.call-start = ((), (), s32[]{:S(2)}) async-start(), calls=%async_computation.1 | async-start | bytes 1114112 | tf_op jit(solution)/shard_map/all_gather | solution.py:76
  6.5 4.8 collective-permute-start
  15.9 49.9 %collective-permute-start.1 = (f32[2,512,512]{2,1,0:T(8,128)}, f32[2,512,512]{2,1,0:T(8,128)}, u32[]{:S(2)}, u32[]{:S(2)}) collective-permute-start(f32[2,512,512]{2,1,0:T(8,128)} %pad_maximum_fusion), channel_id=1, source_target_pairs={{0,2},{2,0},{1,3},{3,1},{4,6},{6,4},{5,7},{7,5},{8,10},{10,8},{9,1... | collective-permute-start | bytes 6291464 | tf_op jit(solution)/shard_map/ppermute | solution.py:15
  77.1 50.5 %collective-permute-start.2 = (f32[2,512,512]{2,1,0:T(8,128)}, f32[2,512,512]{2,1,0:T(8,128)}, u32[]{:S(2)}, u32[]{:S(2)}) collective-permute-start(f32[2,512,512]{2,1,0:T(8,128)} %pad_maximum_fusion.1), channel_id=1, source_target_pairs={{0,4},{4,0},{1,5},{5,1},{2,6},{6,2},{3,7},{7,3},{8,12},{12,8},{9,1... | collective-permute-start | bytes 6291464 | tf_op jit(solution)/shard_map/ppermute | solution.py:15
  138.9 49.6 %collective-permute-start.3 = (f32[2,512,512]{2,1,0:T(8,128)}, f32[2,512,512]{2,1,0:T(8,128)}, u32[]{:S(2)}, u32[]{:S(2)}) collective-permute-start(f32[2,512,512]{2,1,0:T(8,128)} %pad_maximum_fusion.2), channel_id=1, source_target_pairs={{0,8},{8,0},{1,9},{9,1},{2,10},{10,2},{3,11},{11,3},{4,12},{12,4},... | collective-permute-start | bytes 6291464 | tf_op jit(solution)/shard_map/ppermute | solution.py:15
  199.0 128.7 %all-gather.8.cloned.1.call-start = ((), (), s32[]{:S(2)}) async-start(), calls=%async_computation.2 | async-start | bytes 1114112 | tf_op jit(solution)/shard_map/all_gather | solution.py:76
  199.1 10.0 %collective-permute-start.4 = (bf16[2,32,512]{2,1,0:T(8,128)(2,1)}, bf16[2,32,512]{2,1,0:T(8,128)(2,1)S(1)}, u32[]{:S(2)}, u32[]{:S(2)}) collective-permute-start(bf16[2,32,512]{2,1,0:T(8,128)(2,1)} %fusion.50), channel_id=1, source_target_pairs={{0,496},{16,0},{32,16},{48,32},{64,48},{80,64},{96,80},{112,96},{1... | collective-permute-start | bytes 196616 | tf_op jit(solution)/shard_map/ppermute | solution.py:20
  268.5 123.9 %all-gather.10.cloned.1.call-start = ((), (), s32[]{:S(2)}) async-start(), calls=%async_computation.3 | async-start | bytes 1114112 | tf_op jit(solution)/shard_map/all_gather | solution.py:76
  268.6 8.2 %collective-permute-start.5 = (bf16[2,32,512]{2,1,0:T(8,128)(2,1)}, bf16[2,32,512]{2,1,0:T(8,128)(2,1)S(1)}, u32[]{:S(2)}, u32[]{:S(2)}) collective-permute-start(bf16[2,32,512]{2,1,0:T(8,128)(2,1)} %pad_maximum_fusion.3), channel_id=1, source_target_pairs={{0,480},{16,496},{32,0},{48,16},{64,32},{80,48},{96,64},{112,80},{... | collective-permute-start | bytes 196616 | tf_op jit(solution)/shard_map/ppermute | solution.py:20
  333.3 123.9 %all-gather.12.cloned.1.call-start = ((), (), s32[]{:S(2)}) async-start(), calls=%async_computation.4 | async-start | bytes 1114112 | tf_op jit(solution)/shard_map/all_gather | solution.py:76
  333.3 10.3 %collective-permute-start.6 = (bf16[2,32,512]{2,1,0:T(8,128)(2,1)}, bf16[2,32,512]{2,1,0:T(8,128)(2,1)S(1)}, u32[]{:S(2)}, u32[]{:S(2)}) collective-permute-start(bf16[2,32,512]{2,1,0:T(8,128)(2,1)} %pad_maximum_fusion.4), channel_id=1, source_target_pairs={{0,448},{16,464},{32,480},{48,496},{64,0},{80,16},{96,32},{112,48}... | collective-permute-start | bytes 196616 | tf_op jit(solution)/shard_map/ppermute | solution.py:20
  398.1 123.9 %all-gather.14.cloned.1.call-start = ((), (), s32[]{:S(2)}) async-start(), calls=%async_computation.5 | async-start | bytes 1114112 | tf_op jit(solution)/shard_map/all_gather | solution.py:76
  398.1 14.7 %collective-permute-start.7 = (bf16[2,32,512]{2,1,0:T(8,128)(2,1)}, bf16[2,32,512]{2,1,0:T(8,128)(2,1)S(1)}, u32[]{:S(2)}, u32[]{:S(2)}) collective-permute-start(bf16[2,32,512]{2,1,0:T(8,128)(2,1)} %pad_maximum_fusion.5), channel_id=1, source_target_pairs={{0,384},{16,400},{32,416},{48,432},{64,448},{80,464},{96,480},{112... | collective-permute-start | bytes 196616 | tf_op jit(solution)/shard_map/ppermute | solution.py:20
  462.9 15.8 %collective-permute-start.8 = (bf16[2,32,512]{2,1,0:T(8,128)(2,1)}, bf16[2,32,512]{2,1,0:T(8,128)(2,1)S(1)}, u32[]{:S(2)}, u32[]{:S(2)}) collective-permute-start(bf16[2,32,512]{2,1,0:T(8,128)(2,1)} %pad_maximum_fusion.6), channel_id=1, source_target_pairs={{0,256},{16,272},{32,288},{48,304},{64,320},{80,336},{96,352},{112... | collective-permute-start | bytes 196616 | tf_op jit(solution)/shard_map/ppermute | solution.py:20
Sparse Core Ops, SparseCore 0:
  199.1 63.7 all-gather.5
  268.6 58.9 all-gather.7
  333.4 58.9 all-gather.9
  398.2 58.9 all-gather.11
  463.0 58.9 all-gather.13
where the time goes:
time: 566 us; the launch traced here: 564 us
  waiting for transfers between devices  398 us (70%)
  starting transfers between devices  56.8 us (10%)
  matrix products  49.7 us (9%)
  blocking collectives  27.2 us (5%)
  other arithmetic  16.2 us (3%)
  between operations  13.5 us (2%)
    all_gather x5, waiting for transfers between devices, per_device(): lax.all_gather(row_block, 'blk', axis=1, tiled=True)  241 us
    ppermute x4, waiting for transfers between devices, from_partner(): return lax.ppermute(block, axis, route)  140 us
    ppermute x5, starting transfers between devices, passed_along(): lax.ppermute(x, axis, [(i, (i + by) % devices) for i in range(devices)])  41.7 us
    all_to_all x1, blocking collectives, per_device(): lax.all_to_all(row_block[None], 'cuts', split_axis=3, concat_axis=0, tile...  27.2 us
    ppermute x5, waiting for transfers between devices, passed_along(): lax.ppermute(x, axis, [(i, (i + by) % devices) for i in range(devices)])  17.3 us
    ppermute x4, starting transfers between devices, from_partner(): return lax.ppermute(block, axis, route)  14.9 us
  transfers between devices with their start and end apart: 14, of which 14 were waited for; matrix products, arithmetic and copies ran while one was open for 0% of the time, Pallas kernels for 0%

commit v1 on v0

--- a/solution.py
+++ b/solution.py
@@ -76,7 +76,12 @@
             empty_sum, lax.all_gather(row_block, "blk", axis=1, tiled=True), jnp.int32(0)
         )
         row_block = running.astype(jnp.bfloat16)
-    received = lax.all_to_all(row_block[None], "cuts", split_axis=3, concat_axis=0, tiled=True)
+    received = jnp.concatenate(
+        lax.all_to_all(
+            jnp.stack(jnp.split(row_block[None], lax.axis_size("cuts"), axis=3)), "cuts", 0, 0
+        ),
+        axis=0,
+    )
     slice_count = received.shape[0]
     freq_index = jnp.arange(slice_count, dtype=jnp.int32)
     phase_angle = (

time: 566 us -> 568 us (level)
  no operation moved by 1% of the time
where the time goes in v1:
time: 568 us; the launch traced here: 567 us
  waiting for transfers between devices  398 us (70%)
  starting transfers between devices  56.8 us (10%)
  matrix products  49.7 us (9%)
  blocking collectives  27.2 us (5%)
  other arithmetic  18.6 us (3%)
  between operations  13.5 us (2%)
    all_gather x5, waiting for transfers between devices, per_device(): lax.all_gather(row_block, 'blk', axis=1, tiled=True)  241 us
    ppermute x4, waiting for transfers between devices, from_partner(): return lax.ppermute(block, axis, route)  140 us
    ppermute x5, starting transfers between devices, passed_along(): lax.ppermute(x, axis, [(i, (i + by) % devices) for i in range(devices)])  41.7 us
    all_to_all x1, blocking collectives, per_device(): lax.all_to_all(jnp.stack(jnp.split(row_block[None], lax.axis_size('cuts')...  27.2 us
    ppermute x5, waiting for transfers between devices, passed_along(): lax.ppermute(x, axis, [(i, (i + by) % devices) for i in range(devices)])  17.3 us
    ppermute x4, starting transfers between devices, from_partner(): return lax.ppermute(block, axis, route)  14.9 us
  transfers between devices with their start and end apart: 14, of which 14 were waited for; matrix products, arithmetic and copies ran while one was open for 0% of the time, Pallas kernels for 0%

profile of v1, /device:TPU:2, one launch (start us, length us, event | category | flops | bytes accessed | tf_op | source)
XLA Modules:
  0.0 566.9 jit_solution(14910349567148379383)
XLA Ops:
  8.5 2.8 collective-permute-done
  15.9 3.5 collective-permute-start.1
  19.4 46.4 %collective-permute-done.1 = f32[2,512,512]{2,1,0:T(8,128)} collective-permute-done((f32[2,512,512]{2,1,0:T(8,128)}, f32[2,512,512]{2,1,0:T(8,128)}, u32[]{:S(2)}, u32[]{:S(2)}) %collective-permute-start.1) | collective-permute-done | bytes 2097184 | tf_op jit(solution)/shard_map/ppermute | solution.py:15
  65.8 2.3 broadcast_select_fusion.3
  77.1 5.3 collective-permute-start.2
  82.3 45.3 %collective-permute-done.2 = f32[2,512,512]{2,1,0:T(8,128)} collective-permute-done((f32[2,512,512]{2,1,0:T(8,128)}, f32[2,512,512]{2,1,0:T(8,128)}, u32[]{:S(2)}, u32[]{:S(2)}) %collective-permute-start.2) | collective-permute-done | bytes 2097184 | tf_op jit(solution)/shard_map/ppermute | solution.py:15
  127.6 2.3 broadcast_select_fusion.5
  138.9 4.2 collective-permute-start.3
  143.1 45.4 %collective-permute-done.3 = f32[2,512,512]{2,1,0:T(8,128)} collective-permute-done((f32[2,512,512]{2,1,0:T(8,128)}, f32[2,512,512]{2,1,0:T(8,128)}, u32[]{:S(2)}, u32[]{:S(2)}) %collective-permute-start.3) | collective-permute-done | bytes 2097184 | tf_op jit(solution)/shard_map/ppermute | solution.py:15
  188.5 2.3 broadcast_select_fusion.6
  199.1 7.8 %collective-permute-start.4 = (bf16[2,32,512]{2,1,0:T(8,128)(2,1)}, bf16[2,32,512]{2,1,0:T(8,128)(2,1)S(1)}, u32[]{:S(2)}, u32[]{:S(2)}) collective-permute-start(bf16[2,32,512]{2,1,0:T(8,128)(2,1)} %fusion.50), channel_id=1, source_target_pairs={{0,496},{16,0},{32,16},{48,32},{64,48},{80,64},{96,80},{112,96},{1... | collective-permute-start | bytes 196616 | tf_op jit(solution)/shard_map/ppermute | solution.py:20
  209.1 53.8 %all-gather.6.cloned.1.call-done = bf16[2,512,512]{2,1,0:T(8,128)(2,1)} async-done(((bf16[2,32,512]{2,1,0:T(8,128)(2,1)}), bf16[2,512,512]{2,1,0:T(8,128)(2,1)}) %all-gather.6.cloned.1.call-update) | async-done | bytes 1048592 | tf_op jit(solution)/shard_map/all_gather | solution.py:76
  268.6 6.0 %collective-permute-start.5 = (bf16[2,32,512]{2,1,0:T(8,128)(2,1)}, bf16[2,32,512]{2,1,0:T(8,128)(2,1)S(1)}, u32[]{:S(2)}, u32[]{:S(2)}) collective-permute-start(bf16[2,32,512]{2,1,0:T(8,128)(2,1)} %pad_maximum_fusion.3), channel_id=1, source_target_pairs={{0,480},{16,496},{32,0},{48,16},{64,32},{80,48},{96,64},{112,80},{... | collective-permute-start | bytes 196616 | tf_op jit(solution)/shard_map/ppermute | solution.py:20
  276.7 51.0 %all-gather.8.cloned.1.call-done = bf16[2,512,512]{2,1,0:T(8,128)(2,1)} async-done(((bf16[2,32,512]{2,1,0:T(8,128)(2,1)}), bf16[2,512,512]{2,1,0:T(8,128)(2,1)}) %all-gather.8.cloned.1.call-update) | async-done | bytes 1048592 | tf_op jit(solution)/shard_map/all_gather | solution.py:76
  333.3 6.8 %collective-permute-start.6 = (bf16[2,32,512]{2,1,0:T(8,128)(2,1)}, bf16[2,32,512]{2,1,0:T(8,128)(2,1)S(1)}, u32[]{:S(2)}, u32[]{:S(2)}) collective-permute-start(bf16[2,32,512]{2,1,0:T(8,128)(2,1)} %pad_maximum_fusion.4), channel_id=1, source_target_pairs={{0,448},{16,464},{32,480},{48,496},{64,0},{80,16},{96,32},{112,48}... | collective-permute-start | bytes 196616 | tf_op jit(solution)/shard_map/ppermute | solution.py:20
  340.1 3.5 collective-permute-done.6
  343.6 48.8 %all-gather.10.cloned.1.call-done = bf16[2,512,512]{2,1,0:T(8,128)(2,1)} async-done(((bf16[2,32,512]{2,1,0:T(8,128)(2,1)}), bf16[2,512,512]{2,1,0:T(8,128)(2,1)}) %all-gather.10.cloned.1.call-update) | async-done | bytes 1048592 | tf_op jit(solution)/shard_map/all_gather | solution.py:76
  398.1 8.4 %collective-permute-start.7 = (bf16[2,32,512]{2,1,0:T(8,128)(2,1)}, bf16[2,32,512]{2,1,0:T(8,128)(2,1)S(1)}, u32[]{:S(2)}, u32[]{:S(2)}) collective-permute-start(bf16[2,32,512]{2,1,0:T(8,128)(2,1)} %pad_maximum_fusion.5), channel_id=1, source_target_pairs={{0,384},{16,400},{32,416},{48,432},{64,448},{80,464},{96,480},{112... | collective-permute-start | bytes 196616 | tf_op jit(solution)/shard_map/ppermute | solution.py:20
  406.5 6.3 %collective-permute-done.7 = bf16[2,32,512]{2,1,0:T(8,128)(2,1)S(1)} collective-permute-done((bf16[2,32,512]{2,1,0:T(8,128)(2,1)}, bf16[2,32,512]{2,1,0:T(8,128)(2,1)S(1)}, u32[]{:S(2)}, u32[]{:S(2)}) %collective-permute-start.7) | collective-permute-done | bytes 65568 | tf_op jit(solution)/shard_map/ppermute | solution.py:20
  412.8 44.4 %all-gather.12.cloned.1.call-done = bf16[2,512,512]{2,1,0:T(8,128)(2,1)} async-done(((bf16[2,32,512]{2,1,0:T(8,128)(2,1)}), bf16[2,512,512]{2,1,0:T(8,128)(2,1)}) %all-gather.12.cloned.1.call-update) | async-done | bytes 1048592 | tf_op jit(solution)/shard_map/all_gather | solution.py:76
  462.9 12.8 %collective-permute-start.8 = (bf16[2,32,512]{2,1,0:T(8,128)(2,1)}, bf16[2,32,512]{2,1,0:T(8,128)(2,1)S(1)}, u32[]{:S(2)}, u32[]{:S(2)}) collective-permute-start(bf16[2,32,512]{2,1,0:T(8,128)(2,1)} %pad_maximum_fusion.6), channel_id=1, source_target_pairs={{0,256},{16,272},{32,288},{48,304},{64,320},{80,336},{96,352},{112... | collective-permute-start | bytes 196616 | tf_op jit(solution)/shard_map/ppermute | solution.py:20
  475.7 3.0 collective-permute-done.8
  478.7 43.3 %all-gather.14.cloned.1.call-done = bf16[2,512,512]{2,1,0:T(8,128)(2,1)} async-done(((bf16[2,32,512]{2,1,0:T(8,128)(2,1)}), bf16[2,512,512]{2,1,0:T(8,128)(2,1)}) %all-gather.14.cloned.1.call-update) | async-done | bytes 1048592 | tf_op jit(solution)/shard_map/all_gather | solution.py:76
  529.9 27.2 %all_to_all.5 = bf16[32,2,512]{2,1,0:T(2,128)(2,1)S(1)} all-to-all(bf16[32,2,512]{2,1,0:T(2,128)(2,1)S(1)} %reshape.44), channel_id=1, replica_groups=mesh['cuts'=32,'blk'=16] {'cuts'}, dimensions={0} | all-to-all | bytes 131072 | tf_op jit(solution)/shard_map/all_to_all | solution.py:80
  (102 shorter events, 70.5 us)
Async XLA Ops:
  6.5 256.4 %all-gather.6.cloned.1.call-start = ((), (), s32[]{:S(2)}) async-start(), calls=%async_computation.1 | async-start | bytes 1114112 | tf_op jit(solution)/shard_map/all_gather | solution.py:76
  6.5 4.8 collective-permute-start
  15.9 49.9 %collective-permute-start.1 = (f32[2,512,512]{2,1,0:T(8,128)}, f32[2,512,512]{2,1,0:T(8,128)}, u32[]{:S(2)}, u32[]{:S(2)}) collective-permute-start(f32[2,512,512]{2,1,0:T(8,128)} %pad_maximum_fusion), channel_id=1, source_target_pairs={{0,2},{2,0},{1,3},{3,1},{4,6},{6,4},{5,7},{7,5},{8,10},{10,8},{9,1... | collective-permute-start | bytes 6291464 | tf_op jit(solution)/shard_map/ppermute | solution.py:15
  77.1 50.5 %collective-permute-start.2 = (f32[2,512,512]{2,1,0:T(8,128)}, f32[2,512,512]{2,1,0:T(8,128)}, u32[]{:S(2)}, u32[]{:S(2)}) collective-permute-start(f32[2,512,512]{2,1,0:T(8,128)} %pad_maximum_fusion.1), channel_id=1, source_target_pairs={{0,4},{4,0},{1,5},{5,1},{2,6},{6,2},{3,7},{7,3},{8,12},{12,8},{9,1... | collective-permute-start | bytes 6291464 | tf_op jit(solution)/shard_map/ppermute | solution.py:15
  138.9 49.6 %collective-permute-start.3 = (f32[2,512,512]{2,1,0:T(8,128)}, f32[2,512,512]{2,1,0:T(8,128)}, u32[]{:S(2)}, u32[]{:S(2)}) collective-permute-start(f32[2,512,512]{2,1,0:T(8,128)} %pad_maximum_fusion.2), channel_id=1, source_target_pairs={{0,8},{8,0},{1,9},{9,1},{2,10},{10,2},{3,11},{11,3},{4,12},{12,4},... | collective-permute-start | bytes 6291464 | tf_op jit(solution)/shard_map/ppermute | solution.py:15
  199.0 128.7 %all-gather.8.cloned.1.call-start = ((), (), s32[]{:S(2)}) async-start(), calls=%async_computation.2 | async-start | bytes 1114112 | tf_op jit(solution)/shard_map/all_gather | solution.py:76
  199.1 10.0 %collective-permute-start.4 = (bf16[2,32,512]{2,1,0:T(8,128)(2,1)}, bf16[2,32,512]{2,1,0:T(8,128)(2,1)S(1)}, u32[]{:S(2)}, u32[]{:S(2)}) collective-permute-start(bf16[2,32,512]{2,1,0:T(8,128)(2,1)} %fusion.50), channel_id=1, source_target_pairs={{0,496},{16,0},{32,16},{48,32},{64,48},{80,64},{96,80},{112,96},{1... | collective-permute-start | bytes 196616 | tf_op jit(solution)/shard_map/ppermute | solution.py:20
  268.5 123.9 %all-gather.10.cloned.1.call-start = ((), (), s32[]{:S(2)}) async-start(), calls=%async_computation.3 | async-start | bytes 1114112 | tf_op jit(solution)/shard_map/all_gather | solution.py:76
  268.6 8.2 %collective-permute-start.5 = (bf16[2,32,512]{2,1,0:T(8,128)(2,1)}, bf16[2,32,512]{2,1,0:T(8,128)(2,1)S(1)}, u32[]{:S(2)}, u32[]{:S(2)}) collective-permute-start(bf16[2,32,512]{2,1,0:T(8,128)(2,1)} %pad_maximum_fusion.3), channel_id=1, source_target_pairs={{0,480},{16,496},{32,0},{48,16},{64,32},{80,48},{96,64},{112,80},{... | collective-permute-start | bytes 196616 | tf_op jit(solution)/shard_map/ppermute | solution.py:20
  333.3 123.9 %all-gather.12.cloned.1.call-start = ((), (), s32[]{:S(2)}) async-start(), calls=%async_computation.4 | async-start | bytes 1114112 | tf_op jit(solution)/shard_map/all_gather | solution.py:76
  333.3 10.3 %collective-permute-start.6 = (bf16[2,32,512]{2,1,0:T(8,128)(2,1)}, bf16[2,32,512]{2,1,0:T(8,128)(2,1)S(1)}, u32[]{:S(2)}, u32[]{:S(2)}) collective-permute-start(bf16[2,32,512]{2,1,0:T(8,128)(2,1)} %pad_maximum_fusion.4), channel_id=1, source_target_pairs={{0,448},{16,464},{32,480},{48,496},{64,0},{80,16},{96,32},{112,48}... | collective-permute-start | bytes 196616 | tf_op jit(solution)/shard_map/ppermute | solution.py:20
  398.1 123.9 %all-gather.14.cloned.1.call-start = ((), (), s32[]{:S(2)}) async-start(), calls=%async_computation.5 | async-start | bytes 1114112 | tf_op jit(solution)/shard_map/all_gather | solution.py:76
  398.1 14.7 %collective-permute-start.7 = (bf16[2,32,512]{2,1,0:T(8,128)(2,1)}, bf16[2,32,512]{2,1,0:T(8,128)(2,1)S(1)}, u32[]{:S(2)}, u32[]{:S(2)}) collective-permute-start(bf16[2,32,512]{2,1,0:T(8,128)(2,1)} %pad_maximum_fusion.5), channel_id=1, source_target_pairs={{0,384},{16,400},{32,416},{48,432},{64,448},{80,464},{96,480},{112... | collective-permute-start | bytes 196616 | tf_op jit(solution)/shard_map/ppermute | solution.py:20
  462.9 15.8 %collective-permute-start.8 = (bf16[2,32,512]{2,1,0:T(8,128)(2,1)}, bf16[2,32,512]{2,1,0:T(8,128)(2,1)S(1)}, u32[]{:S(2)}, u32[]{:S(2)}) collective-permute-start(bf16[2,32,512]{2,1,0:T(8,128)(2,1)} %pad_maximum_fusion.6), channel_id=1, source_target_pairs={{0,256},{16,272},{32,288},{48,304},{64,320},{80,336},{96,352},{112... | collective-permute-start | bytes 196616 | tf_op jit(solution)/shard_map/ppermute | solution.py:20
Sparse Core Ops, SparseCore 0:
  199.1 63.7 all-gather.5
  268.6 58.9 all-gather.7
  333.4 58.9 all-gather.9
  398.2 58.9 all-gather.11
  463.0 58.9 all-gather.13
